TPU v7x, 256 devices: a whole 4x4x8 slice. The times are simulated.
256 devices in a mesh: row: 16 (over x, y_hi, core), col: 16 (over y_lo, z).
Axes of the slice: x: 4, y: 4 (y_hi: 2, y_lo: 2; y = y_hi * 2 + y_lo), z: 8, core: 2. Of those that a mesh axis runs over, the one named last changes fastest.
Arguments:
- pair_out: bfloat16 [512, 768, 128], P('row', 'col'), may hold values from -6 to 6
- pair_left: bfloat16 [512, 512, 128], P('col', 'row'), may hold values from -6 to 6
- pair_right: bfloat16 [512, 768, 128], P('row', 'col'), may hold values from -6 to 6
- ln_gain: float32 [128], replicated, may hold values from 0.1 to 1.9
- ln_bias: float32 [128], replicated, may hold values from -3 to 3
- w_left: bfloat16 [128, 256], replicated, may hold values from -0.5 to 0.5
- w_right: bfloat16 [128, 256], replicated, may hold values from -0.5 to 0.5
- w_gate: bfloat16 [128, 128], replicated, may hold values from -0.5 to 0.5
- w_out: bfloat16 [128, 128], replicated, may hold values from -0.5 to 0.5
- out_gain: float32 [128], replicated, may hold values from 0.1 to 1.9
- out_bias: float32 [128], replicated, may hold values from -3 to 3
- cotangent: bfloat16 [512, 768, 128], P('row', 'col'), may hold values from -6 to 6
Outputs:
- result: bfloat16 [512, 768, 128], P('row', 'col')
- grad_out: bfloat16 [512, 768, 128], P('row', 'col')
- grad_left: bfloat16 [512, 512, 128], P('col', 'row')
- grad_right: bfloat16 [512, 768, 128], P('row', 'col')
All inputs are finite; a program needn't handle non-finite values.
Results may differ from a plain program's by a relative error of at most 0.025.
Values may be sent and summed in bfloat16 or wider, within the bound.
A program may use at most 128 MiB of HBM per device.

v0:
```python
import jax
import jax.numpy as jnp
from jax import lax
from jax.sharding import PartitionSpec as P


def normalize(values, gain, bias):
    center = values - jnp.mean(values, axis=-1, keepdims=True)
    inverse = lax.rsqrt(jnp.mean(center * center, axis=-1, keepdims=True) + 1e-05)
    standard = center * inverse
    return (standard * gain + bias, standard, inverse)


def norm_back(upstream, standard, inverse, gain):
    scaled = upstream * gain
    return inverse * (
        scaled
        - jnp.mean(scaled, axis=-1, keepdims=True)
        - standard * jnp.mean(scaled * standard, axis=-1, keepdims=True)
    )


def project(pair_tile, gain, bias, weight):
    normed, standard, inverse = normalize(pair_tile.astype(jnp.float32), gain, bias)
    normed = normed.astype(jnp.bfloat16)
    hidden_width = weight.shape[1] // 2
    pre_act = jnp.dot(
        normed.reshape(-1, normed.shape[-1]), weight, preferred_element_type=jnp.float32
    )
    pre_act = pre_act.reshape(pair_tile.shape[:-1] + (2 * hidden_width,))
    gated = (jax.nn.sigmoid(pre_act[..., hidden_width:]) * pre_act[..., :hidden_width]).astype(
        jnp.bfloat16
    )
    return (gated, pre_act, standard, inverse)


def project_back(d_gated, pre_act, standard, inverse, gain, weight):
    hidden_width = weight.shape[1] // 2
    squash = jax.nn.sigmoid(pre_act[..., hidden_width:])
    values_half = pre_act[..., :hidden_width]
    d_pre = jnp.concatenate(
        [d_gated * squash, d_gated * values_half * squash * (1.0 - squash)], axis=-1
    )
    d_pre = d_pre.astype(jnp.bfloat16)
    d_normed = jnp.dot(
        d_pre.reshape(-1, 2 * hidden_width), weight.T, preferred_element_type=jnp.float32
    )
    return norm_back(d_normed.reshape(standard.shape), standard, inverse, gain).astype(jnp.bfloat16)


def per_device(
    pair_out,
    pair_left,
    pair_right,
    ln_gain,
    ln_bias,
    w_left,
    w_right,
    w_gate,
    w_out,
    out_gain,
    out_bias,
    cotangent,
):
    features = pair_out.shape[2]
    hidden_width = w_out.shape[0]
    left_gated, left_pre, left_std, left_inv = project(pair_left, ln_gain, ln_bias, w_left)
    right_gated, right_pre, right_std, right_inv = project(pair_right, ln_gain, ln_bias, w_right)
    left_full = lax.all_gather(left_gated, "col", axis=0, tiled=True)
    right_full = lax.all_gather(right_gated, "row", axis=0, tiled=True)
    triangle = jnp.einsum("kih,kjh->ijh", left_full, right_full, preferred_element_type=jnp.float32)
    tri_normed, tri_std, tri_inv = normalize(triangle, out_gain, out_bias)
    tri_normed = tri_normed.astype(jnp.bfloat16)
    out_normed, out_std, out_inv = normalize(pair_out.astype(jnp.float32), ln_gain, ln_bias)
    out_normed = out_normed.astype(jnp.bfloat16)
    out_gate = jax.nn.sigmoid(
        jnp.dot(out_normed.reshape(-1, features), w_gate, preferred_element_type=jnp.float32)
    )
    out_proj = jnp.dot(
        tri_normed.reshape(-1, hidden_width), w_out, preferred_element_type=jnp.float32
    )
    result = (out_gate * out_proj).astype(jnp.bfloat16).reshape(pair_out.shape)
    upstream = cotangent.reshape(-1, features).astype(jnp.float32)
    d_proj = (upstream * out_gate).astype(jnp.bfloat16)
    d_gate = (upstream * out_proj * out_gate * (1.0 - out_gate)).astype(jnp.bfloat16)
    d_outn = jnp.dot(d_gate, w_gate.T, preferred_element_type=jnp.float32).reshape(pair_out.shape)
    grad_out = norm_back(d_outn, out_std, out_inv, ln_gain).astype(jnp.bfloat16)
    d_trin = jnp.dot(d_proj, w_out.T, preferred_element_type=jnp.float32).reshape(triangle.shape)
    d_triangle = norm_back(d_trin, tri_std, tri_inv, out_gain).astype(jnp.bfloat16)
    d_left = lax.psum_scatter(
        jnp.einsum(
            "ijh,kjh->kih", d_triangle, right_full, preferred_element_type=jnp.float32
        ).astype(jnp.bfloat16),
        "col",
        scatter_dimension=0,
        tiled=True,
    ).astype(jnp.float32)
    d_right = lax.psum_scatter(
        jnp.einsum(
            "ijh,kih->kjh", d_triangle, left_full, preferred_element_type=jnp.float32
        ).astype(jnp.bfloat16),
        "row",
        scatter_dimension=0,
        tiled=True,
    ).astype(jnp.float32)
    grad_left = project_back(d_left, left_pre, left_std, left_inv, ln_gain, w_left)
    grad_right = project_back(d_right, right_pre, right_std, right_inv, ln_gain, w_right)
    return (result, grad_out, grad_left, grad_right)


def solution(mesh):
    return jax.shard_map(
        per_device,
        mesh=mesh,
        in_specs=(
            P("row", "col", None),
            P("col", "row", None),
            P("row", "col", None),
            P(),
            P(),
            P(),
            P(),
            P(),
            P(),
            P(),
            P(),
            P("row", "col", None),
        ),
        out_specs=(
            P("row", "col", None),
            P("row", "col", None),
            P("col", "row", None),
            P("row", "col", None),
        ),
        check_vma=False,
    )
```

profile of v0, /device:TPU:2, one launch (start us, length us, event | category | flops | bytes accessed | tf_op | source)
XLA Modules:
  0.0 410.6 jit_solution(10935491577532320342)
XLA Ops:
  7.2 1.2 convert_reduce_fusion.2
  8.5 1.3 fusion.53
  9.9 1.4 fusion.75
  11.3 1.0 copy-done.6
  12.3 0.8 multiply_convert_fusion.3
  13.2 0.3 convert_reduce_fusion
  13.5 0.5 fusion.20
  14.1 0.6 fusion.68
  14.7 1.1 copy-done.2
  15.8 1.0 multiply_convert_fusion.2
  16.8 0.2 reduce-scatter.3.cloned.1.call-start
  17.1 0.3 convert_reduce_fusion.1
  17.3 0.5 fusion.27
  17.9 0.5 fusion.22
  18.4 0.3 fusion.2
  18.8 0.9 copy-done.8
  19.6 0.5 multiply_reduce_fusion.2
  20.2 2.8 copy.34
  23.0 70.1 %all-gather.5.cloned.1.call-done = bf16[512,32,128]{2,1,0:T(8,128)(2,1)} async-done(((bf16[32,32,128]{2,1,0:T(8,128)(2,1)}), bf16[512,32,128]{2,1,0:T(8,128)(2,1)}) %all-gather.5.cloned.1.call-update) | async-done | bytes 4194320 | tf_op jit(solution)/shard_map/all_gather | solution.py:69
  93.1 23.0 %copy.37 = bf16[512,32,128]{1,0,2:T(8,128)(2,1)} copy(bf16[512,32,128]{2,1,0:T(8,128)(2,1)} %all-gather.5.cloned.1.call-done) | data formatting | bytes 8388608 | tf_op jit(solution)/shard_map/all_gather | solution.py:69
  116.2 46.3 %all-gather.3.cloned.1.call-done = bf16[512,48,128]{2,1,0:T(8,128)(2,1)} async-done(((bf16[32,48,128]{2,1,0:T(8,128)(2,1)}), bf16[512,48,128]{2,1,0:T(8,128)(2,1)}) %all-gather.3.cloned.1.call-update) | async-done | bytes 6291472 | tf_op jit(solution)/shard_map/all_gather | solution.py:70
  162.5 23.1 %copy.31 = bf16[512,48,128]{1,0,2:T(8,128)(2,1)} copy(bf16[512,48,128]{2,1,0:T(8,128)(2,1)} %all-gather.3.cloned.1.call-done) | data formatting | bytes 12582912 | tf_op jit(solution)/shard_map/all_gather | solution.py:70
  185.6 13.3 %bitcast_reduce_fusion = (f32[32,48]{1,0:T(8,128)S(1)}, f32[128,48,32]{1,2,0:T(8,128)S(1)}) fusion(bf16[512,32,128]{1,0,2:T(8,128)(2,1)} %copy.37, bf16[512,48,128]{1,0,2:T(8,128)(2,1)} %copy.31), kind=kOutput, calls=%fused_computation.7 | convolution fusion | flops 201521664 | bytes 11278336 | tf_op jit(solution)/shard_map/kih,kjh->ijh/dot_general | solution.py:71
  198.9 0.3 multiply_reduce_fusion.1
  199.3 1.2 copy-done.1
  200.5 0.4 multiply_reduce_fusion
  200.9 0.2 copy-done.22
  201.1 1.8 multiply_convert_fusion
  202.9 10.8 %fusion.90 = bf16[128,512,32]{1,2,0:T(8,128)(2,1)} fusion(bf16[512,48,128]{1,0,2:T(8,128)(2,1)} %copy.31, bf16[32,48,128]{1,0,2:T(8,128)(2,1)S(1)} %get-tuple-element.8), kind=kOutput, calls=%fused_computation.132 | convolution fusion | flops 201326592 | bytes 10878976 | tf_op jit(solution)/shard_map/ijh,kjh->kih/dot_general | solution.py:91
  213.7 9.1 %copy.36 = bf16[128,512,32]{0,2,1:T(8,128)(2,1)} copy(bf16[128,512,32]{1,2,0:T(8,128)(2,1)} %fusion.90) | data formatting | bytes 8388608 | tf_op jit(solution)/shard_map/ijh,kjh->kih/dot_general | solution.py:91
  222.8 0.3 reduce-scatter.5.cloned.1.call-start
  223.1 11.2 %fusion.91 = bf16[128,512,48]{1,2,0:T(8,128)(2,1)} fusion(bf16[512,32,128]{1,0,2:T(8,128)(2,1)} %copy.37, bf16[32,48,128]{1,0,2:T(8,128)(2,1)S(1)} %get-tuple-element.8), kind=kOutput, calls=%fused_computation.133 | convolution fusion | flops 201326592 | bytes 10878976 | tf_op jit(solution)/shard_map/ijh,kih->kjh/dot_general | solution.py:99
  234.3 9.8 %copy.38 = bf16[128,512,48]{0,2,1:T(8,128)(2,1)} copy(bf16[128,512,48]{1,2,0:T(8,128)(2,1)} %fusion.91) | data formatting | bytes 12582912 | tf_op jit(solution)/shard_map/ijh,kih->kjh/dot_general | solution.py:99
  244.2 1.2 copy-done.13
  245.4 1.1 copy.33
  246.5 1.0 multiply_convert_fusion.1
  247.5 0.5 multiply_reduce_fusion.3
  248.0 0.1 div.75
  248.1 0.7 fusion.23
  248.8 1.7 fusion.26
  250.5 51.9 %reduce-scatter.3.cloned.1.call-done = bf16[32,32,128]{2,1,0:T(8,128)(2,1)} async-done(((bf16[512,32,128]{2,1,0:T(8,128)(2,1)}), bf16[32,32,128]{2,1,0:T(8,128)(2,1)}) %reduce-scatter.3.cloned.1.call-update) | async-done | bytes 262160 | tf_op jit(solution)/shard_map/reduce_scatter | solution.py:90
  302.4 1.2 fusion.54
  303.6 0.8 fusion.89
  304.5 1.3 fusion.52
  305.8 94.3 %reduce-scatter.5.cloned.1.call-done = bf16[32,48,128]{2,1,0:T(8,128)(2,1)} async-done(((bf16[512,48,128]{2,1,0:T(8,128)(2,1)}), bf16[32,48,128]{2,1,0:T(8,128)(2,1)}) %reduce-scatter.5.cloned.1.call-update) | async-done | bytes 393232 | tf_op jit(solution)/shard_map/reduce_scatter | solution.py:98
  400.1 1.3 fusion.28
  401.5 0.9 fusion.88
  402.4 1.7 fusion.19
  (61 shorter events, 0.4 us)
Async XLA Ops:
  7.2 6.9 %copy-start = (bf16[128,256]{1,0:T(8,128)(2,1)S(1)}, bf16[128,256]{1,0:T(8,128)(2,1)}, u32[]{:S(2)}) copy-start(bf16[128,256]{1,0:T(8,128)(2,1)} %param.18) | copy-start | bytes 196612
  7.2 6.0 %copy-start.10 = (bf16[32,48,128]{2,1,0:T(8,128)(2,1)S(1)}, bf16[32,48,128]{2,1,0:T(8,128)(2,1)}, u32[]{:S(2)}) copy-start(bf16[32,48,128]{2,1,0:T(8,128)(2,1)} %param.14) | copy-start | bytes 1179652
  7.2 85.9 %all-gather.5.cloned.1.call-start = ((), (), s32[]{:S(2)}) async-start(), calls=%async_computation.3 | async-start | bytes 4456448 | tf_op jit(solution)/shard_map/all_gather | solution.py:69
  8.5 5.6 %copy-start.19 = (f32[128]{0:T(128)S(1)}, f32[128]{0:T(128)}, u32[]{:S(2)}) copy-start(f32[128]{0:T(128)} %param.15) | copy-start | bytes 1540
  8.5 5.6 %copy-start.20 = (f32[128]{0:T(128)S(1)}, f32[128]{0:T(128)}, u32[]{:S(2)}) copy-start(f32[128]{0:T(128)} %param.16) | copy-start | bytes 1540
  11.3 1.0 copy-start.6
  13.2 149.3 %all-gather.3.cloned.1.call-start = ((), (), s32[]{:S(2)}) async-start(), calls=%async_computation.2 | async-start | bytes 6684672 | tf_op jit(solution)/shard_map/all_gather | solution.py:70
  14.1 3.0 copy-start.4
  14.7 1.2 copy-start.2
  15.8 2.6 copy-start.18
  16.8 285.6 %reduce-scatter.3.cloned.1.call-start = ((), (), s32[]{:S(2)}) async-start(), calls=%async_computation.4 | async-start | bytes 4456448 | tf_op jit(solution)/shard_map/reduce_scatter | solution.py:90
  17.9 1.8 copy-start.14
  17.9 1.7 copy-start.16
  17.9 1.7 copy-start.21
  18.8 0.9 copy-start.8
  198.9 1.6 copy-start.1
  200.5 0.7 copy-start.22
  222.8 177.3 %reduce-scatter.5.cloned.1.call-start = ((), (), s32[]{:S(2)}) async-start(), calls=%async_computation.5 | async-start | bytes 6684672 | tf_op jit(solution)/shard_map/reduce_scatter | solution.py:98
  244.1 1.2 copy-start.13
  244.1 2.3 copy-start.9
  244.2 3.3 copy-start.15
  246.5 1.6 copy-start.5
  248.0 54.4 %copy-start.7 = (f32[32,32,256]{2,1,0:T(8,128)S(1)}, f32[32,32,256]{2,1,0:T(8,128)}, u32[]{:S(2)}) copy-start(f32[32,32,256]{2,1,0:T(8,128)} %copy-done.6) | copy-start | bytes 3145732
  248.1 55.5 %copy-start.12 = (bf16[32,32,128]{2,1,0:T(8,128)(2,1)S(1)}, bf16[32,32,128]{2,1,0:T(8,128)(2,1)}, u32[]{:S(2)}) copy-start(bf16[32,32,128]{2,1,0:T(8,128)(2,1)} %param.13) | copy-start | bytes 786436
  248.1 55.5 %copy-start.17 = (bf16[128,256]{1,0:T(8,128)(2,1)S(1)}, bf16[128,256]{1,0:T(8,128)(2,1)}, u32[]{:S(2)}) copy-start(bf16[128,256]{1,0:T(8,128)(2,1)} %param.17) | copy-start | bytes 196612
  250.5 149.7 %copy-start.3 = (f32[32,48,256]{2,1,0:T(8,128)S(1)}, f32[32,48,256]{2,1,0:T(8,128)}, u32[]{:S(2)}) copy-start(f32[32,48,256]{2,1,0:T(8,128)} %copy-done.2) | copy-start | bytes 4718596
  304.4 97.0 %copy-start.11 = (bf16[32,48,128]{2,1,0:T(8,128)(2,1)S(1)}, bf16[32,48,128]{2,1,0:T(8,128)(2,1)}, u32[]{:S(2)}) copy-start(bf16[32,48,128]{2,1,0:T(8,128)(2,1)} %param.14) | copy-start | bytes 1179652
Sparse Core Ops, SparseCore 0:
  13.3 79.7 all-gather.4
  96.4 66.0 all-gather.2
  223.0 79.3 reduce-scatter.2
  306.7 93.3 reduce-scatter.4
where the time goes:
time: 411 us
  waiting for transfers between devices  263 us (64%)
  local copies, waits for them, and re-layouts  74.8 us (18%)
  matrix products  41.4 us (10%)
  other arithmetic  16.9 us (4%)
  between operations  14.2 us (3%)
    reduce_scatter x1, waiting for transfers between devices, per_device(): lax.psum_scatter(jnp.einsum('ijh,kih->kjh', d_triangle, left_full, prefer...  94.3 us
    all_gather x1, waiting for transfers between devices, per_device(): left_full = lax.all_gather(left_gated, 'col', axis=0, tiled=True)  70.1 us
    reduce_scatter x1, waiting for transfers between devices, per_device(): lax.psum_scatter(jnp.einsum('ijh,kjh->kih', d_triangle, right_full, prefe...  51.9 us
    all_gather x1, waiting for transfers between devices, per_device(): right_full = lax.all_gather(right_gated, 'row', axis=0, tiled=True)  46.3 us
    all_gather x1, local copies, waits for them, and re-layouts, per_device(): right_full = lax.all_gather(right_gated, 'row', axis=0, tiled=True)  23.1 us
    all_gather x1, local copies, waits for them, and re-layouts, per_device(): left_full = lax.all_gather(left_gated, 'col', axis=0, tiled=True)  23 us
    dot_general x1, matrix products, per_device(): jnp.einsum('kih,kjh->ijh', left_full, right_full, preferred_element_type=...  13.3 us
    dot_general x1, matrix products, per_device(): jnp.einsum('ijh,kih->kjh', d_triangle, left_full, preferred_element_type=...  11.2 us
  transfers between devices with their start and end apart: 4, of which 4 were waited for; matrix products, arithmetic and copies ran while one was open for 15% of the time, Pallas kernels for 0%

commit v1 on v0

--- a/solution.py
+++ b/solution.py
@@ -67,7 +67,10 @@
     left_gated, left_pre, left_std, left_inv = project(pair_left, ln_gain, ln_bias, w_left)
     right_gated, right_pre, right_std, right_inv = project(pair_right, ln_gain, ln_bias, w_right)
     left_full = lax.all_gather(left_gated, "col", axis=0, tiled=True)
-    right_full = lax.all_gather(right_gated, "row", axis=0, tiled=True)
+    size = lax.axis_size("row")
+    parts = jnp.stack([right_gated for _ in range(size)])
+    parts = lax.all_to_all(parts, "row", split_axis=0, concat_axis=0)
+    right_full = jnp.concatenate(parts, axis=0)
     triangle = jnp.einsum("kih,kjh->ijh", left_full, right_full, preferred_element_type=jnp.float32)
     tri_normed, tri_std, tri_inv = normalize(triangle, out_gain, out_bias)
     tri_normed = tri_normed.astype(jnp.bfloat16)

time: 411 us -> 392 us (0.954)
  local copies, waits for them, and re-layouts: 74.8 us -> 62.9 us
  matrix products: 41.4 us -> 30.4 us
  starting transfers between devices: 0.56 us -> 8.13 us
    all_to_all x0 -> x1, waiting for transfers between devices: none -> 109 us  [per_device(): parts = lax.all_to_all(parts, 'row', split_axis=0, concat_axis=0)]
    all_gather x1, waiting for transfers between devices: 70.1 us -> 0.01 us  [per_device(): left_full = lax.all_gather(left_gated, 'col', axis=0, tiled=True)]
    all_gather x1 -> x0, waiting for transfers between devices: 46.3 us -> none  [per_device(): right_full = lax.all_gather(right_gated, 'row', axis=0, tiled=True)]
    all_gather x1 -> x0, local copies, waits for them, and re-layouts: 23.1 us -> none  [per_device(): right_full = lax.all_gather(right_gated, 'row', axis=0, tiled=True)]
    reshape x0 -> x1, local copies, waits for them, and re-layouts: none -> 9.68 us  [per_device(): right_full = jnp.concatenate(parts, axis=0)]
    all_to_all x0 -> x1, starting transfers between devices: none -> 7.61 us  [per_device(): parts = lax.all_to_all(parts, 'row', split_axis=0, concat_axis=0)]
    dot_general x1, matrix products: 10.8 us -> 3.16 us  [per_device(): jnp.einsum('ijh,kjh->kih', d_triangle, right_full, preferred_element_type...]
    reduce_scatter x1, waiting for transfers between devices: 51.9 us -> 56.9 us  [per_device(): lax.psum_scatter(jnp.einsum('ijh,kjh->kih', d_triangle, right_full, prefe...]
  transfers between devices with their start and end apart: 4 -> 4, of which waited for: 4 -> 3; matrix products, arithmetic and copies ran while one was open for 15% -> 12% of each run, Pallas kernels for 0% -> 0%
where the time goes in v1:
time: 392 us; the launch traced here: 391 us
  waiting for transfers between devices  260 us (66%)
  local copies, waits for them, and re-layouts  62.9 us (16%)
  matrix products  30.4 us (8%)
  other arithmetic  16.2 us (4%)
  between operations  14.2 us (4%)
  starting transfers between devices  8.13 us (2%)
    all_to_all x1, waiting for transfers between devices, per_device(): parts = lax.all_to_all(parts, 'row', split_axis=0, concat_axis=0)  109 us
    reduce_scatter x1, waiting for transfers between devices, per_device(): lax.psum_scatter(jnp.einsum('ijh,kih->kjh', d_triangle, left_full, prefer...  94 us
    reduce_scatter x1, waiting for transfers between devices, per_device(): lax.psum_scatter(jnp.einsum('ijh,kjh->kih', d_triangle, right_full, prefe...  56.9 us
    all_gather x1, local copies, waits for them, and re-layouts, per_device(): left_full = lax.all_gather(left_gated, 'col', axis=0, tiled=True)  23 us
    dot_general x1, matrix products, per_device(): jnp.einsum('ijh,kih->kjh', d_triangle, left_full, preferred_element_type=...  11.2 us
    dot_general x1, matrix products, per_device(): jnp.einsum('kih,kjh->ijh', left_full, right_full, preferred_element_type=...  9.97 us
    dot_general x1, local copies, waits for them, and re-layouts, per_device(): jnp.einsum('ijh,kih->kjh', d_triangle, left_full, preferred_element_type=...  9.91 us
    reshape x1, local copies, waits for them, and re-layouts, per_device(): right_full = jnp.concatenate(parts, axis=0)  9.68 us
  transfers between devices with their start and end apart: 4, of which 3 were waited for; matrix products, arithmetic and copies ran while one was open for 12% of the time, Pallas kernels for 0%

profile of v1, /device:TPU:2, one launch (start us, length us, event | category | flops | bytes accessed | tf_op | source)
XLA Modules:
  0.0 391.3 jit_solution(14938557190819078959)
XLA Ops:
  7.2 1.2 convert_reduce_fusion.2
  8.5 1.3 fusion.53
  9.8 1.4 fusion.75
  11.3 1.0 copy-done.5
  12.3 0.8 multiply_convert_fusion.3
  13.2 0.3 convert_reduce_fusion
  13.5 0.5 fusion.20
  14.0 0.6 fusion.68
  14.6 1.1 copy-done.1
  15.8 0.2 multiply_convert_fusion.2
  16.0 3.9 stack.2
  19.9 7.6 %all-to-all-start = ((bf16[16,32,48,128]{3,2,1,0:T(8,128)(2,1)}), bf16[16,32,48,128]{3,2,1,0:T(8,128)(2,1)}, u32[]{:S(2)}, u32[]{:S(2)}) async-start(bf16[16,32,48,128]{3,2,1,0:T(8,128)(2,1)} %stack.2), calls=%async_computation | async-start | bytes 12582912 | tf_op jit(solution)/shard_map/all_to_all | solution.py:72
  27.5 0.2 reduce-scatter.3.cloned.1.call-start
  27.7 0.3 convert_reduce_fusion.1
  28.0 0.5 fusion.27
  28.6 0.5 fusion.22
  29.1 0.4 fusion.2
  29.4 0.1 copy-done.13
  29.5 0.5 multiply_reduce_fusion.2
  30.0 0.3 copy-done.7
  30.3 1.8 copy.33
  32.2 108.6 %all-to-all-done = bf16[16,32,48,128]{3,2,1,0:T(8,128)(2,1)} async-done(((bf16[16,32,48,128]{3,2,1,0:T(8,128)(2,1)}), bf16[16,32,48,128]{3,2,1,0:T(8,128)(2,1)}, u32[]{:S(2)}, u32[]{:S(2)}) %all-to-all-start) | async-done | bytes 6291488 | tf_op jit(solution)/shard_map/all_to_all | solution.py:72
  140.8 9.7 %copy.30 = bf16[512,48,128]{0,1,2:T(8,128)(2,1)} copy(bf16[512,48,128]{2,1,0:T(8,128)(2,1)} %bitcast.2) | data formatting | bytes 12582912 | tf_op jit(solution)/shard_map/reshape | solution.py:73
  150.5 23.0 %copy.36 = bf16[512,32,128]{1,0,2:T(8,128)(2,1)} copy(bf16[512,32,128]{2,1,0:T(8,128)(2,1)} %all-gather.2.cloned.1.call-done) | data formatting | bytes 8388608 | tf_op jit(solution)/shard_map/all_gather | solution.py:69
  173.5 10.0 %bitcast_reduce_fusion = (f32[32,48]{1,0:T(8,128)S(1)}, f32[128,48,32]{1,2,0:T(8,128)S(1)}) fusion(bf16[512,48,128]{0,1,2:T(8,128)(2,1)} %copy.30, bf16[512,32,128]{1,0,2:T(8,128)(2,1)} %copy.36), kind=kOutput, calls=%fused_computation.7 | convolution fusion | flops 201521664 | bytes 11278336 | tf_op jit(solution)/shard_map/kih,kjh->ijh/dot_general | solution.py:74
  183.5 0.3 multiply_reduce_fusion.1
  183.9 0.5 multiply_reduce_fusion
  184.4 0.3 copy-done.21
  184.7 1.8 multiply_convert_fusion
  186.6 3.2 fusion.91
  189.7 9.1 %copy.35 = bf16[128,512,32]{0,2,1:T(8,128)(2,1)} copy(bf16[128,512,32]{1,2,0:T(8,128)(2,1)} %fusion.91) | data formatting | bytes 8388608 | tf_op jit(solution)/shard_map/ijh,kjh->kih/dot_general | solution.py:94
  198.9 0.3 reduce-scatter.5.cloned.1.call-start
  199.1 11.2 %fusion.90 = bf16[128,512,48]{1,2,0:T(8,128)(2,1)} fusion(bf16[512,32,128]{1,0,2:T(8,128)(2,1)} %copy.36, bf16[32,48,128]{1,0,2:T(8,128)(2,1)S(1)} %get-tuple-element.8), kind=kOutput, calls=%fused_computation.132 | convolution fusion | flops 201326592 | bytes 10878976 | tf_op jit(solution)/shard_map/ijh,kih->kjh/dot_general | solution.py:102
  210.4 9.9 %copy.37 = bf16[128,512,48]{0,2,1:T(8,128)(2,1)} copy(bf16[128,512,48]{1,2,0:T(8,128)(2,1)} %fusion.90) | data formatting | bytes 12582912 | tf_op jit(solution)/shard_map/ijh,kih->kjh/dot_general | solution.py:102
  220.3 1.2 copy-done.12
  221.5 1.1 copy.32
  222.6 1.0 multiply_convert_fusion.1
  223.6 0.5 multiply_reduce_fusion.3
  224.2 0.7 fusion.23
  224.9 1.7 fusion.26
  226.6 56.9 %reduce-scatter.3.cloned.1.call-done = bf16[32,32,128]{2,1,0:T(8,128)(2,1)} async-done(((bf16[512,32,128]{2,1,0:T(8,128)(2,1)}), bf16[32,32,128]{2,1,0:T(8,128)(2,1)}) %reduce-scatter.3.cloned.1.call-update) | async-done | bytes 262160 | tf_op jit(solution)/shard_map/reduce_scatter | solution.py:93
  283.5 1.2 fusion.54
  284.7 0.8 fusion.89
  285.5 1.3 fusion.52
  286.8 94.0 %reduce-scatter.5.cloned.1.call-done = bf16[32,48,128]{2,1,0:T(8,128)(2,1)} async-done(((bf16[512,48,128]{2,1,0:T(8,128)(2,1)}), bf16[32,48,128]{2,1,0:T(8,128)(2,1)}) %reduce-scatter.5.cloned.1.call-update) | async-done | bytes 393232 | tf_op jit(solution)/shard_map/reduce_scatter | solution.py:101
  380.9 1.3 fusion.28
  382.2 0.9 fusion.88
  383.2 1.7 fusion.19
  (64 shorter events, 0.4 us)
Async XLA Ops:
  7.2 6.8 %copy-start = (bf16[128,256]{1,0:T(8,128)(2,1)S(1)}, bf16[128,256]{1,0:T(8,128)(2,1)}, u32[]{:S(2)}) copy-start(bf16[128,256]{1,0:T(8,128)(2,1)} %param.18) | copy-start | bytes 196612
  7.2 6.0 %copy-start.9 = (bf16[32,48,128]{2,1,0:T(8,128)(2,1)S(1)}, bf16[32,48,128]{2,1,0:T(8,128)(2,1)}, u32[]{:S(2)}) copy-start(bf16[32,48,128]{2,1,0:T(8,128)(2,1)} %param.14) | copy-start | bytes 1179652
  7.2 143.3 %all-gather.2.cloned.1.call-start = ((), (), s32[]{:S(2)}) async-start(), calls=%async_computation.3 | async-start | bytes 4456448 | tf_op jit(solution)/shard_map/all_gather | solution.py:69
  8.5 5.5 %copy-start.18 = (f32[128]{0:T(128)S(1)}, f32[128]{0:T(128)}, u32[]{:S(2)}) copy-start(f32[128]{0:T(128)} %param.15) | copy-start | bytes 1540
  8.5 5.5 %copy-start.19 = (f32[128]{0:T(128)S(1)}, f32[128]{0:T(128)}, u32[]{:S(2)}) copy-start(f32[128]{0:T(128)} %param.16) | copy-start | bytes 1540
  11.3 1.0 copy-start.5
  14.6 1.2 copy-start.1
  19.9 7.8 %copy-start.3 = (bf16[32,48,128]{2,1,0:T(8,128)(2,1)S(1)}, bf16[32,48,128]{2,1,0:T(8,128)(2,1)}, u32[]{:S(2)}) copy-start(bf16[32,48,128]{2,1,0:T(8,128)(2,1)} %param.12) | copy-start | bytes 1179652
  19.9 9.2 %copy-start.17 = (bf16[128,128]{1,0:T(8,128)(2,1)S(1)}, bf16[128,128]{1,0:T(8,128)(2,1)}, u32[]{:S(2)}) copy-start(bf16[128,128]{1,0:T(8,128)(2,1)} %param.19) | copy-start | bytes 98308
  19.9 121.0 %all-to-all-start = ((bf16[16,32,48,128]{3,2,1,0:T(8,128)(2,1)}), bf16[16,32,48,128]{3,2,1,0:T(8,128)(2,1)}, u32[]{:S(2)}, u32[]{:S(2)}) async-start(bf16[16,32,48,128]{3,2,1,0:T(8,128)(2,1)} %stack.2), calls=%async_computation | async-start | bytes 12582912 | tf_op jit(solution)/shard_map/all_to_all | solution.py:72
  27.5 256.0 %reduce-scatter.3.cloned.1.call-start = ((), (), s32[]{:S(2)}) async-start(), calls=%async_computation.4 | async-start | bytes 4456448 | tf_op jit(solution)/shard_map/reduce_scatter | solution.py:93
  28.5 1.0 copy-start.13
  28.5 1.0 copy-start.15
  28.6 1.0 copy-start.20
  29.4 0.9 copy-start.7
  183.5 3.0 slice-start
  183.9 0.8 copy-start.21
  183.9 2.7 slice-start.1
  198.9 182.0 %reduce-scatter.5.cloned.1.call-start = ((), (), s32[]{:S(2)}) async-start(), calls=%async_computation.5 | async-start | bytes 6684672 | tf_op jit(solution)/shard_map/reduce_scatter | solution.py:101
  220.3 1.2 copy-start.12
  220.3 2.3 copy-start.8
  220.3 3.3 copy-start.14
  222.6 1.6 copy-start.4
  224.1 59.4 %copy-start.6 = (f32[32,32,256]{2,1,0:T(8,128)S(1)}, f32[32,32,256]{2,1,0:T(8,128)}, u32[]{:S(2)}) copy-start(f32[32,32,256]{2,1,0:T(8,128)} %copy-done.5) | copy-start | bytes 3145732
  224.2 60.5 %copy-start.11 = (bf16[32,32,128]{2,1,0:T(8,128)(2,1)S(1)}, bf16[32,32,128]{2,1,0:T(8,128)(2,1)}, u32[]{:S(2)}) copy-start(bf16[32,32,128]{2,1,0:T(8,128)(2,1)} %param.13) | copy-start | bytes 786436
  224.2 60.5 %copy-start.16 = (bf16[128,256]{1,0:T(8,128)(2,1)S(1)}, bf16[128,256]{1,0:T(8,128)(2,1)}, u32[]{:S(2)}) copy-start(bf16[128,256]{1,0:T(8,128)(2,1)} %param.17) | copy-start | bytes 196612
  226.6 154.3 %copy-start.2 = (f32[32,48,256]{2,1,0:T(8,128)S(1)}, f32[32,48,256]{2,1,0:T(8,128)}, u32[]{:S(2)}) copy-start(f32[32,48,256]{2,1,0:T(8,128)} %copy-done.1) | copy-start | bytes 4718596
  285.5 96.7 %copy-start.10 = (bf16[32,48,128]{2,1,0:T(8,128)(2,1)S(1)}, bf16[32,48,128]{2,1,0:T(8,128)(2,1)}, u32[]{:S(2)}) copy-start(bf16[32,48,128]{2,1,0:T(8,128)(2,1)} %param.14) | copy-start | bytes 1179652
Sparse Core Ops, SparseCore 0:
  13.3 102.5 all-gather.1
  199.0 84.4 reduce-scatter.2
  287.9 92.9 reduce-scatter.4
